TPU v7x, 32 devices: a whole 2x2x4 slice. The times are simulated.
32 devices in a mesh: shards: 4 (over z), context: 2 (over y), tensor: 4 (over x, core).
Axes of the slice: x: 2, y: 2, z: 4, core: 2. Of those that a mesh axis runs over, the one named last changes fastest.
Arguments:
- tokens: bfloat16 [8, 2048, 768], P('shards', 'context'), may hold values from -6 to 6
- norm_gain: bfloat16 [768], replicated, may hold values from 0.099609375 to 1.8984375
- w_z: bfloat16 [768, 1536], P('shards', 'tensor'), may hold values from -0.21875 to 0.21875
- w_x: bfloat16 [768, 1536], P('shards', 'tensor'), may hold values from -0.21875 to 0.21875
- w_bc: bfloat16 [768, 256], P('shards'), may hold values from -0.21875 to 0.21875
- w_dt: bfloat16 [768, 24], P('shards', 'tensor'), may hold values from -0.21875 to 0.21875
- conv_x: bfloat16 [4, 1536], P(None, 'tensor'), may hold values from -3 to 3
- conv_bc: bfloat16 [4, 256], replicated, may hold values from -3 to 3
- dt_bias: float32 [24], P('tensor'), may hold values from -3 to -0.5
- a_log: float32 [24], P('tensor'), may hold values from -10 to -3
- skip: float32 [24], P('tensor'), may hold values from 0.5 to 1.5
- gate_gain: bfloat16 [1536], P('tensor'), may hold values from 0.099609375 to 1.8984375
- w_out: bfloat16 [1536, 768], P('tensor', 'shards'), may hold values from -0.15625 to 0.15625
- cotangent: bfloat16 [8, 2048, 768], P('shards', 'context'), may hold values from -6 to 6
Outputs:
- mixed: bfloat16 [8, 2048, 768], P('shards', 'context')
- grad_tokens: float32 [8, 2048, 768], P('shards', 'context')
- grad_norm_gain: float32 [768], replicated
- grad_w_z: float32 [768, 1536], P(('shards', 'context'), 'tensor')
- grad_w_x: float32 [768, 1536], P(('shards', 'context'), 'tensor')
- grad_w_bc: float32 [768, 256], P(('shards', 'context'))
- grad_w_dt: float32 [768, 24], P(('shards', 'context'), 'tensor')
- grad_conv_x: float32 [4, 1536], P(None, 'tensor')
- grad_conv_bc: float32 [4, 256], replicated
- grad_dt_bias: float32 [24], P('tensor')
- grad_a_log: float32 [24], P('tensor')
- grad_skip: float32 [24], P('tensor')
- grad_gate_gain: float32 [1536], P('tensor')
- grad_w_out: float32 [1536, 768], P('tensor', ('shards', 'context'))
All inputs are finite; a program needn't handle non-finite values.
Results may differ from a plain program's by a relative error of at most 0.012.
The roundings to bfloat16 on the way count: a program that leaves them out, or rounds other values in their place, can miss the bound.
Values may be sent and summed in bfloat16 or wider, within the bound.
A program may use at most 192 MiB of HBM per device.

v0:
```python
import jax
import jax.numpy as jnp
from jax import lax
from jax.sharding import PartitionSpec as P

BLOCK = 256
INNER = 1536


epsilon = 1e-05
highest = lax.Precision.HIGHEST


def from_behind(value, axis, steps):
    count = lax.axis_size(axis)
    first, last = (max(0, -steps), min(count, count - steps))
    return lax.ppermute(value, axis, [(source, source + steps) for source in range(first, last)])


def prefix(part, axis, combine, identity, reverse):
    count = lax.axis_size(axis)
    place = lax.axis_index(axis)
    ahead = count - 1 - place if reverse else place
    gathered = jax.tree.map(lambda a: lax.all_gather(a, axis), part)
    state = jax.tree.map(lambda a, e: jnp.zeros_like(a) + jnp.asarray(e, a.dtype), part, identity)

    def one(step, state):
        source = count - 1 - step if reverse else step
        return combine(
            state, jax.tree.map(lambda a: lax.dynamic_index_in_dim(a, source, 0, False), gathered)
        )

    return lax.fori_loop(0, ahead, one, state)


def product(left, right):
    return jnp.dot(left, right, preferred_element_type=jnp.float32)


def product_transposed(left, right):
    return lax.dot_general(
        left, right, (((1,), (1,)), ((), ())), preferred_element_type=jnp.float32
    )


def product_over_rows(left, right):
    return lax.dot_general(
        left, right, (((0,), (0,)), ((), ())), preferred_element_type=jnp.float32
    )


def depthwise(signal, edge_rows, weights):
    tap_count = weights.shape[0]
    span_len = signal.shape[1]
    padded = jnp.concatenate([edge_rows, signal], axis=1).astype(jnp.float32)
    wide_taps = weights.astype(jnp.float32)
    total = wide_taps[0] * padded[:, 0:span_len]
    for offset in range(1, tap_count):
        total = total + wide_taps[offset] * padded[:, offset : offset + span_len]
    return (total, padded)


def depthwise_back(grad_conv, edge_rows, weights, padded):
    tap_count = weights.shape[0]
    span_len = grad_conv.shape[1]
    wide_taps = weights.astype(jnp.float32)
    extended = jnp.concatenate([grad_conv, edge_rows], axis=1)
    grad_signal = wide_taps[tap_count - 1] * extended[:, 0:span_len]
    for offset in range(1, tap_count):
        grad_signal = (
            grad_signal
            + wide_taps[tap_count - 1 - offset] * extended[:, offset : offset + span_len]
        )
    grad_taps = jnp.stack(
        [
            jnp.sum(grad_conv * padded[:, offset : offset + span_len], axis=(0, 1))
            for offset in range(tap_count)
        ]
    )
    return (grad_signal, grad_taps)


def silu_slope(value):
    sigma = jax.nn.sigmoid(value)
    return sigma * (1.0 + value * (1.0 - sigma))


def chain(earlier, later):
    return (earlier[0] * later[0], later[0][:, :, None, None] * earlier[1] + later[1])


def on_device(
    tokens,
    norm_gain,
    w_z,
    w_x,
    w_bc,
    w_dt,
    conv_x,
    conv_bc,
    dt_bias,
    a_log,
    skip,
    gate_gain,
    w_out,
    cotangent,
):
    seq_count, span_len, model_width = tokens.shape
    row_count = seq_count * span_len
    head_count = dt_bias.shape[0]
    state_size = w_bc.shape[1] // 2
    tap_count = conv_x.shape[0]
    block_count = span_len // BLOCK
    full_z, full_x, full_bc, full_dt, full_out = (
        lax.all_gather(w_z, "shards", axis=0, tiled=True),
        lax.all_gather(w_x, "shards", axis=0, tiled=True),
        lax.all_gather(w_bc, "shards", axis=0, tiled=True),
        lax.all_gather(w_dt, "shards", axis=0, tiled=True),
        lax.all_gather(w_out, "shards", axis=1, tiled=True),
    )
    inner_width = full_z.shape[1]
    head_width = inner_width // head_count
    flat_rows = tokens.reshape(row_count, model_width).astype(jnp.float32)
    row_scale = lax.rsqrt(jnp.mean(flat_rows * flat_rows, axis=1, keepdims=True) + epsilon)
    unit_rows = flat_rows * row_scale
    gain_input = norm_gain.astype(jnp.float32)
    normed = (unit_rows * gain_input).astype(jnp.bfloat16)
    gate_value = product(normed, full_z)
    x_pre = product(normed, full_x).astype(jnp.bfloat16).reshape(seq_count, span_len, inner_width)
    bc_pre = (
        product(normed, full_bc).astype(jnp.bfloat16).reshape(seq_count, span_len, 2 * state_size)
    )
    dt_raw = product(normed, full_dt)
    x_edge, bc_edge = from_behind(
        (x_pre[:, span_len - tap_count + 1 :], bc_pre[:, span_len - tap_count + 1 :]), "context", 1
    )
    x_conv, x_padded = depthwise(x_pre, x_edge, conv_x)
    bc_conv, bc_padded = depthwise(bc_pre, bc_edge, conv_bc)
    x_act = jax.nn.silu(x_conv).astype(jnp.bfloat16)
    bc_act = jax.nn.silu(bc_conv).astype(jnp.bfloat16)
    x_blocks = x_act.reshape(seq_count, block_count, BLOCK, head_count, head_width)
    b_in = bc_act[:, :, :state_size].reshape(seq_count, block_count, BLOCK, state_size)
    c_in = bc_act[:, :, state_size:].reshape(seq_count, block_count, BLOCK, state_size)
    pre_step = dt_raw + dt_bias
    step_size = jax.nn.softplus(pre_step)
    rate = -jnp.exp(a_log)
    step_heads = jnp.transpose(
        step_size.reshape(seq_count, block_count, BLOCK, head_count), (0, 1, 3, 2)
    )
    decay_sum = jnp.cumsum(step_heads * rate[:, None], axis=3)
    last_sum = decay_sum[..., -1]
    causal = lax.broadcasted_iota(jnp.int32, (BLOCK, BLOCK), 0) >= lax.broadcasted_iota(
        jnp.int32, (BLOCK, BLOCK), 1
    )
    gram_matrix = jnp.einsum("scin,scjn->scij", c_in, b_in, preferred_element_type=jnp.float32)
    spacing = decay_sum[..., :, None] - decay_sum[..., None, :]
    within = jnp.where(causal, jnp.exp(jnp.where(causal, spacing, 0.0)), 0.0)
    masked_within = within * step_heads[..., None, :]
    mix_full = gram_matrix[:, :, None] * masked_within
    mixing = mix_full.astype(jnp.bfloat16)
    intra = jnp.einsum("schij,scjhp->scihp", mixing, x_blocks, preferred_element_type=jnp.float32)
    toward = jnp.exp(last_sum[..., None] - decay_sum) * step_heads
    b_wide = b_in.astype(jnp.float32)
    loaded = (b_wide[:, :, None] * toward[..., None]).astype(jnp.bfloat16)
    fresh_state = jnp.einsum(
        "schjn,scjhp->schnp", loaded, x_blocks, preferred_element_type=jnp.float32
    )
    carried = jnp.zeros((seq_count, head_count, state_size, head_width), jnp.float32)
    entering = []
    for index in range(block_count):
        entering.append(carried)
        carried = jnp.exp(last_sum[:, index])[:, :, None, None] * carried + fresh_state[:, index]
    device_total = jnp.sum(last_sum, axis=1)
    device_decay = jnp.exp(device_total)
    identity = (jnp.ones_like(device_decay), jnp.zeros_like(carried))
    incoming = prefix((device_decay, carried), "context", chain, identity, False)[1]
    after_sum = jnp.cumsum(last_sum, axis=1)
    start_decay = jnp.exp(after_sum - last_sum)
    enter_true = jnp.stack(entering, axis=1) + start_decay[..., None, None] * incoming[:, None]
    c_wide = c_in.astype(jnp.float32)
    reached = jnp.einsum("scin,schnp->scihp", c_wide, enter_true, precision=highest)
    growth = jnp.exp(jnp.transpose(decay_sum, (0, 1, 3, 2)))
    x_wide = x_blocks.astype(jnp.float32)
    scanned = intra + growth[..., None] * reached + skip[:, None] * x_wide
    scanned = scanned.reshape(row_count, inner_width)
    sigma_gate = jax.nn.sigmoid(gate_value)
    silu_gate = gate_value * sigma_gate
    gated_out = scanned * silu_gate
    gain_gate = gate_gain.astype(jnp.float32)
    weighted = (gated_out * gain_gate).astype(jnp.bfloat16)
    partial_value = product(weighted, full_out)
    square_sums = jnp.sum(gated_out * gated_out, axis=1)
    grad_rows = cotangent.reshape(row_count, model_width).astype(jnp.float32)
    projected, squares = lax.psum((partial_value, square_sums), "tensor")
    out_scale = lax.rsqrt(squares / INNER + epsilon)
    mixed_flat = (flat_rows + projected * out_scale[:, None]).astype(jnp.bfloat16)
    grad_scale = jnp.sum(grad_rows * projected, axis=1)
    grad_spread = -0.5 * grad_scale * out_scale * out_scale * out_scale
    mixed = mixed_flat.reshape(seq_count, span_len, model_width)
    grad_proj = (grad_rows * out_scale[:, None]).astype(jnp.bfloat16)
    grad_weighted = product_transposed(grad_proj, full_out)
    grad_w_out = product_over_rows(weighted, grad_proj)
    grad_gate_gain = jnp.sum(grad_weighted * gated_out, axis=0)
    grad_gated = grad_weighted * gain_gate + 2.0 / INNER * grad_spread[:, None] * gated_out
    grad_scanned = (grad_gated * silu_gate).astype(jnp.bfloat16)
    grad_gate = (
        grad_gated * scanned * sigma_gate * (1.0 + gate_value * (1.0 - sigma_gate))
    ).astype(jnp.bfloat16)
    grad_blocks = grad_scanned.reshape(seq_count, block_count, BLOCK, head_count, head_width)
    grad_wide = grad_blocks.astype(jnp.float32)
    grad_skip = jnp.sum(grad_wide * x_wide, axis=(0, 1, 2, 4))
    grad_reached = grad_wide * growth[..., None]
    from_output = jnp.einsum("scin,scihp->schnp", c_wide, grad_reached, precision=highest)
    carried_back = jnp.zeros_like(carried)
    leaving = []
    for index in range(block_count - 1, -1, -1):
        leaving.append(carried_back)
        carried_back = (
            from_output[:, index] + jnp.exp(last_sum[:, index])[:, :, None, None] * carried_back
        )
    outgoing = prefix((device_decay, carried_back), "context", chain, identity, True)[1]
    end_decay = jnp.exp(device_total[:, None] - after_sum)
    leave_true = jnp.stack(leaving[::-1], axis=1) + end_decay[..., None, None] * outgoing[:, None]
    grad_x_blocks = skip[:, None] * grad_wide
    grad_x_blocks = grad_x_blocks + jnp.einsum(
        "schij,scihp->scjhp", mixing, grad_blocks, preferred_element_type=jnp.float32
    )
    grad_x_blocks = grad_x_blocks + jnp.einsum(
        "schjn,schnp->scjhp", loaded.astype(jnp.float32), leave_true, precision=highest
    )
    grad_mix = jnp.einsum(
        "scihp,scjhp->schij", grad_blocks, x_blocks, preferred_element_type=jnp.float32
    )
    grad_gram = jnp.sum(grad_mix * masked_within, axis=2)
    grad_step = jnp.sum(grad_mix * gram_matrix[:, :, None] * within, axis=3)
    spread_term = grad_mix * mix_full
    grad_cum = jnp.sum(spread_term, axis=4) - jnp.sum(spread_term, axis=3)
    grad_c_in = jnp.einsum("scij,scjn->scin", grad_gram, b_wide, precision=highest)
    grad_c_in = grad_c_in + jnp.einsum(
        "scihp,schnp->scin", grad_reached, enter_true, precision=highest
    )
    grad_b_in = jnp.einsum("scij,scin->scjn", grad_gram, c_wide, precision=highest)
    grad_cum = grad_cum + jnp.transpose(jnp.sum(grad_reached * reached, axis=4), (0, 1, 3, 2))
    grad_last = jnp.sum(leave_true * enter_true, axis=(3, 4)) * jnp.exp(last_sum)
    grad_loaded = jnp.einsum("scjhp,schnp->schjn", x_wide, leave_true, precision=highest)
    grad_b_in = grad_b_in + jnp.sum(grad_loaded * toward[..., None], axis=2)
    touch = jnp.sum(grad_loaded * b_wide[:, :, None], axis=4)
    touch_part = touch * toward
    grad_step = grad_step + touch * jnp.exp(last_sum[..., None] - decay_sum)
    grad_last = grad_last + jnp.sum(touch_part, axis=3)
    grad_cum = (grad_cum - touch_part).at[..., -1].add(grad_last)
    grad_log = jnp.flip(jnp.cumsum(jnp.flip(grad_cum, 3), axis=3), 3)
    grad_step = grad_step + grad_log * rate[:, None]
    grad_a_log = jnp.sum(grad_log * step_heads, axis=(0, 1, 3)) * rate
    grad_pre = jnp.transpose(grad_step, (0, 1, 3, 2)).reshape(
        row_count, head_count
    ) * jax.nn.sigmoid(pre_step)
    grad_dt_bias = jnp.sum(grad_pre, axis=0)
    grad_dt_raw = grad_pre.astype(jnp.bfloat16)
    grad_x_conv = grad_x_blocks.reshape(seq_count, span_len, inner_width) * silu_slope(x_conv)
    grad_bc_act = jnp.concatenate([grad_b_in, grad_c_in], axis=3).reshape(
        seq_count, span_len, 2 * state_size
    )
    grad_bc_conv = grad_bc_act * silu_slope(bc_conv)
    x_next, bc_next = from_behind(
        (grad_x_conv[:, : tap_count - 1], grad_bc_conv[:, : tap_count - 1]), "context", -1
    )
    grad_x_signal, grad_conv_x = depthwise_back(grad_x_conv, x_next, conv_x, x_padded)
    grad_bc_signal, conv_bc_part = depthwise_back(grad_bc_conv, bc_next, conv_bc, bc_padded)
    grad_x_pre = grad_x_signal.reshape(row_count, inner_width).astype(jnp.bfloat16)
    normed_part = (
        product_transposed(grad_gate, full_z)
        + product_transposed(grad_x_pre, full_x)
        + product_transposed(grad_dt_raw, full_dt)
    )
    grad_normed, grad_bc_total, grad_conv_bc = lax.psum(
        (normed_part, grad_bc_signal.reshape(row_count, 2 * state_size), conv_bc_part), "tensor"
    )
    grad_bc_pre = grad_bc_total.astype(jnp.bfloat16)
    grad_normed = grad_normed + product_transposed(grad_bc_pre, full_bc)
    grad_norm_gain = jnp.sum(grad_normed * unit_rows, axis=0)
    grad_unit = grad_normed * gain_input
    grad_tokens = grad_rows + row_scale * (
        grad_unit - unit_rows * jnp.mean(grad_unit * unit_rows, axis=1, keepdims=True)
    )
    grad_w_z = product_over_rows(normed, grad_gate)
    grad_w_x = product_over_rows(normed, grad_x_pre)
    grad_w_bc = product_over_rows(normed, grad_bc_pre)
    grad_w_dt = product_over_rows(normed, grad_dt_raw)
    final_z, final_x, final_bc, final_dt, final_out = (
        lax.psum_scatter(grad_w_z, ("shards", "context"), scatter_dimension=0, tiled=True),
        lax.psum_scatter(grad_w_x, ("shards", "context"), scatter_dimension=0, tiled=True),
        lax.psum_scatter(grad_w_bc, ("shards", "context"), scatter_dimension=0, tiled=True),
        lax.psum_scatter(grad_w_dt, ("shards", "context"), scatter_dimension=0, tiled=True),
        lax.psum_scatter(grad_w_out, ("shards", "context"), scatter_dimension=1, tiled=True),
    )
    small_sums = lax.psum(
        (
            grad_norm_gain,
            grad_conv_x,
            grad_conv_bc,
            grad_dt_bias,
            grad_a_log,
            grad_skip,
            grad_gate_gain,
        ),
        ("shards", "context"),
    )
    return (
        mixed,
        grad_tokens.reshape(seq_count, span_len, model_width),
        small_sums[0],
        final_z,
        final_x,
        final_bc,
        final_dt,
        small_sums[1],
        small_sums[2],
        small_sums[3],
        small_sums[4],
        small_sums[5],
        small_sums[6],
        final_out,
    )


def solution(mesh):
    placed = (
        P("shards", "context", None),
        P(),
        P("shards", "tensor"),
        P("shards", "tensor"),
        P("shards", None),
        P("shards", "tensor"),
        P(None, "tensor"),
        P(),
        P("tensor"),
        P("tensor"),
        P("tensor"),
        P("tensor"),
        P("tensor", "shards"),
        P("shards", "context", None),
    )
    return jax.shard_map(
        on_device,
        mesh=mesh,
        in_specs=placed,
        out_specs=(
            P("shards", "context", None),
            P("shards", "context", None),
            P(),
            P(("shards", "context"), "tensor"),
            P(("shards", "context"), "tensor"),
            P(("shards", "context"), None),
            P(("shards", "context"), "tensor"),
            P(None, "tensor"),
            P(),
            P("tensor"),
            P("tensor"),
            P("tensor"),
            P("tensor"),
            P("tensor", ("shards", "context")),
        ),
        check_vma=False,
    )
```

profile of v0, /device:TPU:0, one launch (start us, length us, event | category | flops | bytes accessed | tf_op | source)
XLA Modules:
  0.0 976.1 jit_solution(12639786496169600148)
XLA Ops:
  10.6 16.4 %all_gather.30 = bf16[768,256]{1,0:T(8,128)(2,1)S(1)} all-gather(bf16[192,256]{1,0:T(8,128)(2,1)} %param.24), channel_id=1, replica_groups=mesh['shards'=4,'context'=2,'tensor'=4] {'shards'}, dimensions={0}, use_global_device_ids=true | all-gather | bytes 491520 | tf_op jit(solution)/shard_map/all_gather | solution.py:117
  33.3 16.6 %all_gather.29 = bf16[768,384]{1,0:T(8,128)(2,1)S(1)} all-gather(bf16[192,384]{1,0:T(8,128)(2,1)S(1)} %copy-done.54), channel_id=1, replica_groups=mesh['shards'=4,'context'=2,'tensor'=4] {'shards'}, dimensions={0}, use_global_device_ids=true | all-gather | bytes 737280 | tf_op jit(solution)/shard_map/all_gather | solution.py:116
  58.7 13.1 %all-gather.1 = bf16[4,192,6]{1,2,0:T(8,128)(2,1)S(1)} all-gather(bf16[1,192,6]{1,2,0:T(8,128)(2,1)S(1)} %bitcast.294), channel_id=1, replica_groups=mesh['shards'=4,'context'=2,'tensor'=4] {'shards'}, dimensions={0}, use_global_device_ids=true | all-gather | bytes 11520 | tf_op jit(solution)/shard_map/all_gather | solution.py:118
  75.1 14.4 %reduce-window.14 = f32[2,4,6,2,128]{4,3,2,1,0:T(2,128)S(1)} reduce-window(f32[2,4,6,2,128]{4,3,2,1,0:T(2,128)S(1)} %copy.436, f32[]{:T(128)} %constant.104.clone.1), window={size=1x1x1x1x128 pad=0_0x0_0x0_0x0_0x127_0}, to_apply=%region_1.2 | reduce-window | flops 1560576 | bytes 98308 | tf_op jit(solution)/shard_map/reduce-window
  93.7 18.0 %all_gather.34 = bf16[768,384]{1,0:T(8,128)(2,1)} all-gather(bf16[192,384]{1,0:T(8,128)(2,1)} %param.22), channel_id=1, replica_groups=mesh['shards'=4,'context'=2,'tensor'=4] {'shards'}, dimensions={0}, use_global_device_ids=true | all-gather | bytes 737280 | tf_op jit(solution)/shard_map/all_gather | solution.py:115
  111.7 16.1 %all_gather.35 = bf16[384,768]{0,1:T(8,128)(2,1)} all-gather(bf16[384,192]{0,1:T(8,128)(2,1)} %param.32), channel_id=1, replica_groups=mesh['shards'=4,'context'=2,'tensor'=4] {'shards'}, dimensions={1}, use_global_device_ids=true | all-gather | bytes 737280 | tf_op jit(solution)/shard_map/all_gather | solution.py:119
  158.9 8.6 all_gather.33
  193.6 7.7 multiply_reduce_fusion.10
  218.9 113.3 %all-reduce.6.cloned.1.call-done = f32[2048,768]{1,0:T(8,128)} async-done(((f32[2048,768]{1,0:T(8,128)}), f32[2048,768]{1,0:T(8,128)}) %all-reduce.6.cloned.1.call-update) | async-done | bytes 6291472 | tf_op jit(solution)/shard_map/psum | solution.py:194
  332.3 7.0 fusion.7
  368.7 12.1 %fusion.4 = (f32[2,4,6,256]{3,2,1,0:T(8,128)}, f32[2,4,6,256]{3,2,1,0:T(8,128)}, f32[2,4,6,256]{3,2,1,0:T(8,128)}, f32[2,4,256,256]{3,2,1,0:T(8,128)}) fusion(f32[2,4,6,256]{3,2,1,0:T(8,128)S(1)} %copy-done.64, f32[2,4,6,256]{3,2,1,0:T(8,128)S(1)} %copy-done.62, f32[2,4,256,256]{3,2,1,0:T(8,128)S(1)} %copy-done.42, pred[256,256]{1,0:T(8,128)(4,1)S(1)} %copy-done.66, ...), kind=kOutput, calls=%fused_computation.16 | convolution fusion | flops 442986496 | bytes 7651328 | tf_op jit(solution)/shard_map/scihp,scjhp->schij/dot_general | solution.py:231
  385.3 11.8 %all_gather.36 = f32[2,2,6,128,64]{3,4,2,1,0:T(8,128)} all-gather(f32[1,2,6,128,64]{3,4,2,1,0:T(8,128)S(1)} %fusion.88), channel_id=1, replica_groups=mesh['shards'=4,'context'=2,'tensor'=4] {'context'}, dimensions={0}, use_global_device_ids=true | all-gather | bytes 1179648 | tf_op jit(solution)/shard_map/all_gather | solution.py:24
  398.1 6.4 while.28
  452.4 25.6 %reduce-window.16 = f32[2,4,6,2,128]{4,3,2,1,0:T(2,128)} reduce-window(f32[2,4,6,2,128]{4,3,2,1,0:T(2,128)} %copy.489, f32[]{:T(128)} %constant.104.clone.1), window={size=1x1x1x1x128 pad=0_0x0_0x0_0x0_0x127_0}, to_apply=%region_20.21 | reduce-window | flops 1560576 | bytes 98308 | tf_op jit(solution)/shard_map/reduce-window.2
  495.8 6.2 multiply_reduce_fusion.8
  542.6 42.4 %all-reduce.9 = (bf16[2048,256]{1,0:T(8,128)(2,1)}, f32[4,256]{1,0:T(4,128)}) all-reduce(f32[2048,256]{1,0:T(8,128)} %bitcast.250, f32[4,256]{1,0:T(4,128)S(1)} %pad_maximum_fusion.4), channel_id=1, replica_groups=mesh['shards'=4,'context'=2,'tensor'=4] {'tensor'}, use_global_device_ids=true, to_apply=%region_25.26 | all-reduce | flops 525312 | bytes 3153920 | tf_op jit(solution)/shard_map/psum | solution.py:276
  614.0 86.9 %all-reduce.8.cloned.1.call-done = f32[2048,768]{1,0:T(8,128)} async-done(((f32[2048,768]{1,0:T(8,128)}), f32[2048,768]{1,0:T(8,128)}) %all-reduce.8.cloned.1.call-update) | async-done | bytes 6291472 | tf_op jit(solution)/shard_map/psum | solution.py:276
  700.9 6.8 fusion.16
  707.7 38.5 %all-reduce = (f32[768]{0:T(1024)}, f32[4,384]{1,0:T(4,128)}, f32[4,256]{1,0:T(4,128)}, f32[6]{0:T(128)}, f32[6]{0:T(128)}, /*index=5*/f32[6]{0:T(128)}, f32[384]{0:T(512)}) all-reduce(f32[768]{0:T(1024)S(1)} %get-tuple-element.240, ...), channel_id=1, replica_groups=mesh['shards'=4,'context'=2,'tensor'=4] {'shards','context'}, use_global_device_ids=true, to_apply=%region_28.29 | all-reduce | flops 3730 | bytes 29840 | tf_op jit(solution)/shard_map/psum | solution.py:297
  746.8 6.3 convert_add_fusion
  753.1 14.2 %reduce-scatter.12.cloned.1.call-done = f32[96,256]{1,0:T(8,128)} async-done(((f32[768,256]{1,0:T(8,128)}), f32[96,256]{1,0:T(8,128)}) %reduce-scatter.12.cloned.1.call-update) | async-done | bytes 98320 | tf_op jit(solution)/shard_map/reduce_scatter | solution.py:293
  767.3 67.3 %reduce-scatter.14.cloned.1.call-done = f32[384,96]{0,1:T(8,128)} async-done(((f32[384,768]{0,1:T(8,128)}), f32[384,96]{0,1:T(8,128)}) %reduce-scatter.14.cloned.1.call-update) | async-done | bytes 147472 | tf_op jit(solution)/shard_map/reduce_scatter | solution.py:295
  834.6 67.1 %reduce-scatter.8.cloned.1.call-done = f32[96,384]{1,0:T(8,128)} async-done(((f32[768,384]{1,0:T(8,128)}), f32[96,384]{1,0:T(8,128)}) %reduce-scatter.8.cloned.1.call-update) | async-done | bytes 147472 | tf_op jit(solution)/shard_map/reduce_scatter | solution.py:291
  901.7 67.3 %reduce-scatter.10.cloned.1.call-done = f32[96,384]{1,0:T(8,128)} async-done(((f32[768,384]{1,0:T(8,128)}), f32[96,384]{1,0:T(8,128)}) %reduce-scatter.10.cloned.1.call-update) | async-done | bytes 147472 | tf_op jit(solution)/shard_map/reduce_scatter | solution.py:292
  (406 shorter events, 276.7 us)
Async XLA Ops:
  7.2 325.1 %all-reduce.6.cloned.1.call-start = ((), (), s32[]{:S(2)}) async-start(), calls=%async_computation.5 | async-start | bytes 12582912 | tf_op jit(solution)/shard_map/psum | solution.py:194
  29.9 106.5 %collective-permute-start.1 = (bf16[2,3,256]{2,1,0:T(4,128)(2,1)S(1)}, bf16[2,3,256]{2,1,0:T(4,128)(2,1)S(1)}, u32[]{:S(2)}, u32[]{:S(2)}) collective-permute-start(bf16[2,3,256]{2,1,0:T(4,128)(2,1)S(1)} %slice.238), channel_id=1, source_target_pairs={{0,4},{1,5},{2,6},{3,7},{8,12},{9,13},{10,14},{11,15},{16,20},{17,... | collective-permute-start | bytes 9224 | tf_op jit(solution)/shard_map/ppermute | solution.py:17
  56.7 87.7 %collective-permute-start = (bf16[2,3,384]{1,2,0:T(8,128)(2,1)S(1)}, bf16[2,3,384]{1,2,0:T(8,128)(2,1)}, u32[]{:S(2)}, u32[]{:S(2)}) collective-permute-start(bf16[2,3,384]{1,2,0:T(8,128)(2,1)S(1)} %slice.229), channel_id=1, source_target_pairs={{0,4},{1,5},{2,6},{3,7},{8,12},{9,13},{10,14},{11,15},{16,20},{17,... | collective-permute-start | bytes 13832 | tf_op jit(solution)/shard_map/ppermute | solution.py:17
  90.7 45.2 %copy-start.21 = (f32[2,4,6,256]{2,1,3,0:T(4,128)}, f32[2,4,6,256]{2,1,3,0:T(4,128)S(1)}, u32[]{:S(2)}) copy-start(f32[2,4,6,256]{2,1,3,0:T(4,128)S(1)} %copy.445) | copy-start | bytes 147460
  90.7 45.2 %copy-start.112 = (bf16[384]{0:T(512)(128)(2,1)S(1)}, bf16[384]{0:T(512)(128)(2,1)}, u32[]{:S(2)}) copy-start(bf16[384]{0:T(512)(128)(2,1)} %param.31) | copy-start | bytes 2308
  91.1 46.8 %copy-start.22 = (f32[2,4,6,256]{2,1,3,0:T(4,128)}, f32[2,4,6,256]{2,1,3,0:T(4,128)S(1)}, u32[]{:S(2)}) copy-start(f32[2,4,6,256]{2,1,3,0:T(4,128)S(1)} %bitcast_multiply_fusion.3) | copy-start | bytes 147460
  91.7 42.8 %copy-start.90 = (f32[2,1,6]{2,1,0:T(1,128)}, f32[2,1,6]{2,1,0:T(1,128)S(1)}, u32[]{:S(2)}) copy-start(f32[2,1,6]{2,1,0:T(1,128)S(1)} %get-tuple-element.328) | copy-start | bytes 148
  91.7 67.0 %copy-start.71 = (f32[2,1,6]{2,1,0:T(1,128)}, f32[2,1,6]{2,1,0:T(1,128)S(1)}, u32[]{:S(2)}) copy-start(f32[2,1,6]{2,1,0:T(1,128)S(1)} %get-tuple-element.326) | copy-start | bytes 148
  92.4 48.0 %copy-start.94 = (f32[1,256]{1,0:T(1,128)}, f32[1,256]{1,0:T(1,128)S(1)}, u32[]{:S(2)}) copy-start(f32[1,256]{1,0:T(1,128)S(1)} %get-tuple-element.329) | copy-start | bytes 3076
  92.4 48.0 %copy-start.96 = (f32[1,256]{1,0:T(1,128)}, f32[1,256]{1,0:T(1,128)S(1)}, u32[]{:S(2)}) copy-start(f32[1,256]{1,0:T(1,128)S(1)} %get-tuple-element.330) | copy-start | bytes 3076
  92.4 48.0 %copy-start.98 = (f32[1,256]{1,0:T(1,128)}, f32[1,256]{1,0:T(1,128)S(1)}, u32[]{:S(2)}) copy-start(f32[1,256]{1,0:T(1,128)S(1)} %get-tuple-element.331) | copy-start | bytes 3076
  92.5 48.0 %copy-start.100 = (f32[1,256]{1,0:T(1,128)}, f32[1,256]{1,0:T(1,128)S(1)}, u32[]{:S(2)}) copy-start(f32[1,256]{1,0:T(1,128)S(1)} %get-tuple-element.332) | copy-start | bytes 3076
  207.5 405.0 %reduce-scatter.16.cloned.1.call-start = ((), (), s32[]{:S(2)}) async-start(), calls=%async_computation.11 | async-start | bytes 442368
  447.8 37.2 %copy-start.107 = (f32[6]{0:T(128)S(1)}, f32[6]{0:T(128)}, u32[]{:S(2)}) copy-start(f32[6]{0:T(128)} %copy-done.106) | copy-start | bytes 76
  503.0 13.1 %collective-permute-start.2 = (f32[2,3,384]{1,2,0:T(8,128)}, f32[2,3,384]{1,2,0:T(8,128)S(1)}, u32[]{:S(2)}, u32[]{:S(2)}) collective-permute-start(f32[2,3,384]{1,2,0:T(8,128)} %slice.263), channel_id=1, source_target_pairs={{4,0},{5,1},{6,2},{7,3},{12,8},{13,9},{14,10},{15,11},{20,16},{21,... | collective-permute-start | bytes 27656 | tf_op jit(solution)/shard_map/ppermute | solution.py:17
  516.0 184.9 %all-reduce.8.cloned.1.call-start = ((), (), s32[]{:S(2)}) async-start(), calls=%async_computation.6 | async-start | bytes 12582912 | tf_op jit(solution)/shard_map/psum | solution.py:276
  529.8 237.5 %reduce-scatter.12.cloned.1.call-start = ((), (), s32[]{:S(2)}) async-start(), calls=%async_computation.9 | async-start | bytes 884736 | tf_op jit(solution)/shard_map/reduce_scatter | solution.py:293
  534.8 5.6 collective-permute-start.3
  536.1 48.9 %copy-start.7 = (bf16[2048,768]{1,0:T(8,128)(2,1)S(1)}, bf16[2048,768]{1,0:T(8,128)(2,1)}, u32[]{:S(2)}) copy-start(bf16[2048,768]{1,0:T(8,128)(2,1)} %copy-done.4) | copy-start | bytes 9437188
  588.1 246.5 %reduce-scatter.14.cloned.1.call-start = ((), (), s32[]{:S(2)}) async-start(), calls=%async_computation.10 | async-start | bytes 1327104 | tf_op jit(solution)/shard_map/reduce_scatter | solution.py:295
  594.0 307.7 %reduce-scatter.8.cloned.1.call-start = ((), (), s32[]{:S(2)}) async-start(), calls=%async_computation.7 | async-start | bytes 1327104 | tf_op jit(solution)/shard_map/reduce_scatter | solution.py:291
  599.5 369.5 %reduce-scatter.10.cloned.1.call-start = ((), (), s32[]{:S(2)}) async-start(), calls=%async_computation.8 | async-start | bytes 1327104 | tf_op jit(solution)/shard_map/reduce_scatter | solution.py:292
  599.5 101.4 %copy-start.47 = (bf16[768,256]{1,0:T(8,128)(2,1)S(1)}, bf16[768,256]{1,0:T(8,128)(2,1)}, u32[]{:S(2)}) copy-start(bf16[768,256]{1,0:T(8,128)(2,1)} %copy-done.46) | copy-start | bytes 1179652
  599.6 101.4 %copy-start.56 = (f32[1,8,2,128]{3,1,2,0:T(8,128)S(1)}, f32[1,8,2,128]{3,1,2,0:T(8,128)}, u32[]{:S(2)}) copy-start(f32[1,8,2,128]{3,1,2,0:T(8,128)} %copy-done.55) | copy-start | bytes 24580
  (104 other events, 602.1 us)
Sparse Core Ops, SparseCore 0:
  207.7 124.5 all-reduce.5
  516.1 63.1 reduce-scatter.15
  582.3 118.5 all-reduce.7
  704.6 62.6 reduce-scatter.11
  771.5 63.0 reduce-scatter.13
  838.8 62.8 reduce-scatter.7
  906.1 62.9 reduce-scatter.9
where the time goes:
time: 984 us; the launch traced here: 976 us
  waiting for transfers between devices  421 us (43%)
  blocking collectives  192 us (20%)
  other arithmetic  121 us (12%)
  local copies, waits for them, and re-layouts  109 us (11%)
  matrix products  109 us (11%)
  between operations  15.6 us (2%)
    psum x1, waiting for transfers between devices, on_device(): projected, squares = lax.psum((partial_value, square_sums), 'tensor')  113 us
    psum x1, waiting for transfers between devices, on_device(): lax.psum((normed_part, grad_bc_signal.reshape(row_count, 2 * state_size),...  86.9 us
    reduce_scatter x1, waiting for transfers between devices, on_device(): lax.psum_scatter(grad_w_out, ('shards', 'context'), scatter_dimension=1,...  67.3 us
    reduce_scatter x1, waiting for transfers between devices, on_device(): lax.psum_scatter(grad_w_x, ('shards', 'context'), scatter_dimension=0, ti...  67.3 us
    reduce_scatter x1, waiting for transfers between devices, on_device(): lax.psum_scatter(grad_w_z, ('shards', 'context'), scatter_dimension=0, ti...  67.1 us
    psum x1, blocking collectives, on_device(): lax.psum((normed_part, grad_bc_signal.reshape(row_count, 2 * state_size),...  42.4 us
    another operation x6, other arithmetic  41.7 us
    psum x1, blocking collectives, on_device(): lax.psum((grad_norm_gain, grad_conv_x, grad_conv_bc, grad_dt_bias, grad_a...  38.5 us
  transfers between devices with their start and end apart: 11, of which 7 were waited for; matrix products, arithmetic and copies ran while one was open for 12% of the time, Pallas kernels for 0%

commit v1 on v0

--- a/solution.py
+++ b/solution.py
@@ -15,22 +15,6 @@
     count = lax.axis_size(axis)
     first, last = (max(0, -steps), min(count, count - steps))
     return lax.ppermute(value, axis, [(source, source + steps) for source in range(first, last)])
-
-
-def prefix(part, axis, combine, identity, reverse):
-    count = lax.axis_size(axis)
-    place = lax.axis_index(axis)
-    ahead = count - 1 - place if reverse else place
-    gathered = jax.tree.map(lambda a: lax.all_gather(a, axis), part)
-    state = jax.tree.map(lambda a, e: jnp.zeros_like(a) + jnp.asarray(e, a.dtype), part, identity)
-
-    def one(step, state):
-        source = count - 1 - step if reverse else step
-        return combine(
-            state, jax.tree.map(lambda a: lax.dynamic_index_in_dim(a, source, 0, False), gathered)
-        )
-
-    return lax.fori_loop(0, ahead, one, state)
 
 
 def product(left, right):
@@ -83,10 +67,6 @@
 def silu_slope(value):
     sigma = jax.nn.sigmoid(value)
     return sigma * (1.0 + value * (1.0 - sigma))
-
-
-def chain(earlier, later):
-    return (earlier[0] * later[0], later[0][:, :, None, None] * earlier[1] + later[1])
 
 
 def on_device(
@@ -111,13 +91,17 @@
     state_size = w_bc.shape[1] // 2
     tap_count = conv_x.shape[0]
     block_count = span_len // BLOCK
-    full_z, full_x, full_bc, full_dt, full_out = (
-        lax.all_gather(w_z, "shards", axis=0, tiled=True),
-        lax.all_gather(w_x, "shards", axis=0, tiled=True),
-        lax.all_gather(w_bc, "shards", axis=0, tiled=True),
-        lax.all_gather(w_dt, "shards", axis=0, tiled=True),
-        lax.all_gather(w_out, "shards", axis=1, tiled=True),
-    )
+    inner_part = w_z.shape[1]
+    packed = jnp.concatenate(
+        [w_x, w_bc, jnp.pad(w_dt, ((0, 0), (0, 128 - head_count))), w_z, w_out.T], axis=1
+    )
+    full = lax.all_gather(packed, "shards", axis=0, tiled=True)
+    at_z = inner_part + 2 * state_size + 128
+    full_x = full[:, :inner_part]
+    full_bc = full[:, inner_part : inner_part + 2 * state_size]
+    full_dt = full[:, inner_part + 2 * state_size : inner_part + 2 * state_size + head_count]
+    full_z = full[:, at_z : at_z + inner_part]
+    out_t = full[:, at_z + inner_part :]
     inner_width = full_z.shape[1]
     head_width = inner_width // head_count
     flat_rows = tokens.reshape(row_count, model_width).astype(jnp.float32)
@@ -125,15 +109,14 @@
     unit_rows = flat_rows * row_scale
     gain_input = norm_gain.astype(jnp.float32)
     normed = (unit_rows * gain_input).astype(jnp.bfloat16)
-    gate_value = product(normed, full_z)
-    x_pre = product(normed, full_x).astype(jnp.bfloat16).reshape(seq_count, span_len, inner_width)
-    bc_pre = (
-        product(normed, full_bc).astype(jnp.bfloat16).reshape(seq_count, span_len, 2 * state_size)
-    )
-    dt_raw = product(normed, full_dt)
-    x_edge, bc_edge = from_behind(
-        (x_pre[:, span_len - tap_count + 1 :], bc_pre[:, span_len - tap_count + 1 :]), "context", 1
-    )
+    fronts = product(normed, full[:, : at_z + inner_part])
+    gate_value = fronts[:, at_z:]
+    pre = fronts[:, : inner_part + 2 * state_size].astype(jnp.bfloat16)
+    pre = pre.reshape(seq_count, span_len, inner_part + 2 * state_size)
+    x_pre, bc_pre = pre[..., :inner_part], pre[..., inner_part:]
+    dt_raw = fronts[:, inner_part + 2 * state_size : inner_part + 2 * state_size + head_count]
+    edge = from_behind(pre[:, span_len - tap_count + 1 :], "context", 1)
+    x_edge, bc_edge = edge[..., :inner_part], edge[..., inner_part:]
     x_conv, x_padded = depthwise(x_pre, x_edge, conv_x)
     bc_conv, bc_padded = depthwise(bc_pre, bc_edge, conv_bc)
     x_act = jax.nn.silu(x_conv).astype(jnp.bfloat16)
@@ -147,7 +130,8 @@
     step_heads = jnp.transpose(
         step_size.reshape(seq_count, block_count, BLOCK, head_count), (0, 1, 3, 2)
     )
-    decay_sum = jnp.cumsum(step_heads * rate[:, None], axis=3)
+    lower = jnp.tril(jnp.ones((BLOCK, BLOCK), jnp.float32))
+    decay_sum = jnp.einsum("schj,ij->schi", step_heads * rate[:, None], lower, precision=highest)
     last_sum = decay_sum[..., -1]
     causal = lax.broadcasted_iota(jnp.int32, (BLOCK, BLOCK), 0) >= lax.broadcasted_iota(
         jnp.int32, (BLOCK, BLOCK), 1
@@ -172,8 +156,7 @@
         carried = jnp.exp(last_sum[:, index])[:, :, None, None] * carried + fresh_state[:, index]
     device_total = jnp.sum(last_sum, axis=1)
     device_decay = jnp.exp(device_total)
-    identity = (jnp.ones_like(device_decay), jnp.zeros_like(carried))
-    incoming = prefix((device_decay, carried), "context", chain, identity, False)[1]
+    incoming = from_behind(carried, "context", 1)
     after_sum = jnp.cumsum(last_sum, axis=1)
     start_decay = jnp.exp(after_sum - last_sum)
     enter_true = jnp.stack(entering, axis=1) + start_decay[..., None, None] * incoming[:, None]
@@ -188,24 +171,42 @@
     gated_out = scanned * silu_gate
     gain_gate = gate_gain.astype(jnp.float32)
     weighted = (gated_out * gain_gate).astype(jnp.bfloat16)
-    partial_value = product(weighted, full_out)
+    partial_value = product_transposed(weighted, out_t)
     square_sums = jnp.sum(gated_out * gated_out, axis=1)
     grad_rows = cotangent.reshape(row_count, model_width).astype(jnp.float32)
-    projected, squares = lax.psum((partial_value, square_sums), "tensor")
+    scale_part = jnp.sum(grad_rows * partial_value, axis=1)
+    squares, grad_scale = lax.psum(jnp.stack([square_sums, scale_part]), "tensor")
+    own_rows = row_count // lax.axis_size("tensor")
+    own_at = lax.axis_index("tensor") * own_rows
+
+    def own(value):
+        return lax.dynamic_slice_in_dim(value, own_at, own_rows, 0)
+
     out_scale = lax.rsqrt(squares / INNER + epsilon)
-    mixed_flat = (flat_rows + projected * out_scale[:, None]).astype(jnp.bfloat16)
-    grad_scale = jnp.sum(grad_rows * projected, axis=1)
+    own_projected = lax.psum_scatter(
+        partial_value.astype(jnp.bfloat16), "tensor", scatter_dimension=0, tiled=True
+    ).astype(jnp.float32)
+    own_mixed = (own(flat_rows) + own_projected * own(out_scale)[:, None]).astype(jnp.bfloat16)
+    mixed = lax.all_gather(own_mixed, "tensor", axis=0, tiled=True).reshape(tokens.shape)
     grad_spread = -0.5 * grad_scale * out_scale * out_scale * out_scale
-    mixed = mixed_flat.reshape(seq_count, span_len, model_width)
     grad_proj = (grad_rows * out_scale[:, None]).astype(jnp.bfloat16)
-    grad_weighted = product_transposed(grad_proj, full_out)
-    grad_w_out = product_over_rows(weighted, grad_proj)
+    grad_weighted = product(grad_proj, out_t)
+    grad_out_t = product_over_rows(grad_proj, weighted)
+    final_out = lax.psum_scatter(
+        grad_out_t.astype(jnp.bfloat16), ("shards", "context"), scatter_dimension=0, tiled=True
+    ).astype(jnp.float32).T
     grad_gate_gain = jnp.sum(grad_weighted * gated_out, axis=0)
     grad_gated = grad_weighted * gain_gate + 2.0 / INNER * grad_spread[:, None] * gated_out
     grad_scanned = (grad_gated * silu_gate).astype(jnp.bfloat16)
     grad_gate = (
         grad_gated * scanned * sigma_gate * (1.0 + gate_value * (1.0 - sigma_gate))
     ).astype(jnp.bfloat16)
+    final_z = lax.psum_scatter(
+        product_over_rows(normed, grad_gate).astype(jnp.bfloat16),
+        ("shards", "context"),
+        scatter_dimension=0,
+        tiled=True,
+    ).astype(jnp.float32)
     grad_blocks = grad_scanned.reshape(seq_count, block_count, BLOCK, head_count, head_width)
     grad_wide = grad_blocks.astype(jnp.float32)
     grad_skip = jnp.sum(grad_wide * x_wide, axis=(0, 1, 2, 4))
@@ -218,7 +219,7 @@
         carried_back = (
             from_output[:, index] + jnp.exp(last_sum[:, index])[:, :, None, None] * carried_back
         )
-    outgoing = prefix((device_decay, carried_back), "context", chain, identity, True)[1]
+    outgoing = from_behind(carried_back, "context", -1)
     end_decay = jnp.exp(device_total[:, None] - after_sum)
     leave_true = jnp.stack(leaving[::-1], axis=1) + end_decay[..., None, None] * outgoing[:, None]
     grad_x_blocks = skip[:, None] * grad_wide
@@ -249,7 +250,7 @@
     grad_step = grad_step + touch * jnp.exp(last_sum[..., None] - decay_sum)
     grad_last = grad_last + jnp.sum(touch_part, axis=3)
     grad_cum = (grad_cum - touch_part).at[..., -1].add(grad_last)
-    grad_log = jnp.flip(jnp.cumsum(jnp.flip(grad_cum, 3), axis=3), 3)
+    grad_log = jnp.einsum("schi,ij->schj", grad_cum, lower, precision=highest)
     grad_step = grad_step + grad_log * rate[:, None]
     grad_a_log = jnp.sum(grad_log * step_heads, axis=(0, 1, 3)) * rate
     grad_pre = jnp.transpose(grad_step, (0, 1, 3, 2)).reshape(
@@ -262,9 +263,14 @@
         seq_count, span_len, 2 * state_size
     )
     grad_bc_conv = grad_bc_act * silu_slope(bc_conv)
-    x_next, bc_next = from_behind(
-        (grad_x_conv[:, : tap_count - 1], grad_bc_conv[:, : tap_count - 1]), "context", -1
-    )
+    following = from_behind(
+        jnp.concatenate(
+            [grad_x_conv[:, : tap_count - 1], grad_bc_conv[:, : tap_count - 1]], axis=2
+        ),
+        "context",
+        -1,
+    )
+    x_next, bc_next = following[..., :inner_width], following[..., inner_width:]
     grad_x_signal, grad_conv_x = depthwise_back(grad_x_conv, x_next, conv_x, x_padded)
     grad_bc_signal, conv_bc_part = depthwise_back(grad_bc_conv, bc_next, conv_bc, bc_padded)
     grad_x_pre = grad_x_signal.reshape(row_count, inner_width).astype(jnp.bfloat16)
@@ -273,53 +279,70 @@
         + product_transposed(grad_x_pre, full_x)
         + product_transposed(grad_dt_raw, full_dt)
     )
-    grad_normed, grad_bc_total, grad_conv_bc = lax.psum(
-        (normed_part, grad_bc_signal.reshape(row_count, 2 * state_size), conv_bc_part), "tensor"
-    )
-    grad_bc_pre = grad_bc_total.astype(jnp.bfloat16)
-    grad_normed = grad_normed + product_transposed(grad_bc_pre, full_bc)
-    grad_norm_gain = jnp.sum(grad_normed * unit_rows, axis=0)
-    grad_unit = grad_normed * gain_input
-    grad_tokens = grad_rows + row_scale * (
-        grad_unit - unit_rows * jnp.mean(grad_unit * unit_rows, axis=1, keepdims=True)
-    )
-    grad_w_z = product_over_rows(normed, grad_gate)
-    grad_w_x = product_over_rows(normed, grad_x_pre)
-    grad_w_bc = product_over_rows(normed, grad_bc_pre)
-    grad_w_dt = product_over_rows(normed, grad_dt_raw)
-    final_z, final_x, final_bc, final_dt, final_out = (
-        lax.psum_scatter(grad_w_z, ("shards", "context"), scatter_dimension=0, tiled=True),
-        lax.psum_scatter(grad_w_x, ("shards", "context"), scatter_dimension=0, tiled=True),
-        lax.psum_scatter(grad_w_bc, ("shards", "context"), scatter_dimension=0, tiled=True),
-        lax.psum_scatter(grad_w_dt, ("shards", "context"), scatter_dimension=0, tiled=True),
-        lax.psum_scatter(grad_w_out, ("shards", "context"), scatter_dimension=1, tiled=True),
-    )
-    small_sums = lax.psum(
-        (
-            grad_norm_gain,
-            grad_conv_x,
-            grad_conv_bc,
-            grad_dt_bias,
-            grad_a_log,
-            grad_skip,
-            grad_gate_gain,
-        ),
+    own_bc = lax.psum_scatter(
+        grad_bc_signal.reshape(row_count, 2 * state_size),
+        "tensor",
+        scatter_dimension=0,
+        tiled=True,
+    ).astype(jnp.bfloat16)
+    own_grad = lax.psum_scatter(
+        normed_part.astype(jnp.bfloat16), "tensor", scatter_dimension=0, tiled=True
+    ).astype(jnp.float32)
+    own_grad = own_grad + product_transposed(own_bc, full_bc)
+    own_unit = own(unit_rows)
+    grad_norm_gain = jnp.sum(own_grad * own_unit, axis=0)
+    grad_unit = own_grad * gain_input
+    own_tokens = own(grad_rows) + own(row_scale) * (
+        grad_unit - own_unit * jnp.mean(grad_unit * own_unit, axis=1, keepdims=True)
+    )
+    grad_tokens = lax.all_gather(
+        own_tokens.astype(jnp.bfloat16), "tensor", axis=0, tiled=True
+    ).astype(jnp.float32)
+    back = jnp.concatenate([grad_x_pre, grad_dt_raw], axis=1)
+    grad_back = product_over_rows(normed, back)
+    grad_w_bc = product_over_rows(own(normed), own_bc)
+    final_back = lax.psum_scatter(
+        jnp.concatenate([grad_back, grad_w_bc], axis=1).astype(jnp.bfloat16),
         ("shards", "context"),
-    )
+        scatter_dimension=0,
+        tiled=True,
+    ).astype(jnp.float32)
+    final_x = final_back[:, :inner_width]
+    final_dt = final_back[:, inner_width : inner_width + head_count]
+    whole = jnp.concatenate([grad_norm_gain, conv_bc_part.reshape(-1)])
+    by_tensor = jnp.concatenate(
+        [grad_conv_x.reshape(-1), grad_gate_gain, grad_dt_bias, grad_a_log, grad_skip]
+    )
+    final_bc = lax.psum(final_back[:, inner_width + head_count :], "tensor")
+    places = lax.axis_size("tensor")
+    here = lax.axis_index("tensor")
+    spread_out = jnp.zeros((places, by_tensor.shape[0]), jnp.float32).at[here].set(by_tensor)
+    sums = lax.psum(
+        jnp.concatenate([whole, spread_out.reshape(-1)]), ("shards", "context", "tensor")
+    )
+    norm_sum = sums[:model_width]
+    conv_bc_sum = sums[model_width : whole.shape[0]].reshape(conv_bc.shape)
+    mine = lax.dynamic_index_in_dim(
+        sums[whole.shape[0] :].reshape(places, -1), here, 0, keepdims=False
+    )
+    at = tap_count * inner_width
+    conv_x_sum = mine[:at].reshape(tap_count, inner_width)
+    gate_gain_sum = mine[at : at + inner_width]
+    heads_sum = mine[at + inner_width :].reshape(3, head_count)
     return (
         mixed,
         grad_tokens.reshape(seq_count, span_len, model_width),
-        small_sums[0],
+        norm_sum,
         final_z,
         final_x,
         final_bc,
         final_dt,
-        small_sums[1],
-        small_sums[2],
-        small_sums[3],
-        small_sums[4],
-        small_sums[5],
-        small_sums[6],
+        conv_x_sum,
+        conv_bc_sum,
+        heads_sum[0],
+        heads_sum[1],
+        heads_sum[2],
+        gate_gain_sum,
         final_out,
     )
 

time: 984 us -> 702 us (0.71)
  blocking collectives: 192 us -> 51.3 us
  waiting for transfers between devices: 421 us -> 319 us
  other arithmetic: 121 us -> 83.6 us
  matrix products: 109 us -> 97.2 us
    psum x2 -> x1, waiting for transfers between devices: 200 us -> 29.7 us  [on_device(): final_bc = lax.psum(final_back[:, inner_width + head_count:], 'tensor')]
    all_gather x8 -> x0, blocking collectives: 105 us -> none  [the longest x3 24.8 us: prefix(): gathered = jax.tree.map(lambda a: lax.all_gather(a, axis), part)]
    another operation x8 -> x3, other arithmetic: 43.1 us -> 1.98 us
    unnamed x8 -> x11, waiting for transfers between devices: 0.12 us -> 40.8 us
    all_gather x0 -> x3, waiting for transfers between devices: none -> 40 us  [the longest x1 28.4 us: on_device(): full = lax.all_gather(packed, 'shards', axis=0, tiled=True)]
    psum x3 -> x2, blocking collectives: 86.7 us -> 51.3 us  [the longest x1 39.9 us: on_device(): lax.psum(jnp.concatenate([whole, spread_out.reshape(-1)]), ('shards', 'co...]
    reduce_scatter x4 -> x5, waiting for transfers between devices: 216 us -> 196 us  [the longest x1 62.8 us: on_device(): lax.psum_scatter(grad_out_t.astype(jnp.bfloat16), ('shards', 'context'),...]
    unnamed x239 -> x263, local copies, waits for them, and re-layouts: 16.6 us -> 31.5 us
  transfers between devices with their start and end apart: 11 -> 14, of which waited for: 7 -> 11; matrix products, arithmetic and copies ran while one was open for 12% -> 18% of each run, Pallas kernels for 0% -> 0%
where the time goes in v1:
time: 702 us; the launch traced here: 692 us
  waiting for transfers between devices  319 us (45%)
  local copies, waits for them, and re-layouts  114 us (16%)
  matrix products  97.2 us (14%)
  other arithmetic  83.6 us (12%)
  blocking collectives  51.3 us (7%)
  between operations  16.1 us (2%)
  starting transfers between devices  9.96 us (1%)
    reduce_scatter x1, waiting for transfers between devices, on_device(): lax.psum_scatter(grad_out_t.astype(jnp.bfloat16), ('shards', 'context'),...  62.8 us
    reduce_scatter x1, waiting for transfers between devices, on_device(): lax.psum_scatter(product_over_rows(normed, grad_gate).astype(jnp.bfloat16...  57.7 us
    unnamed x11, waiting for transfers between devices  40.8 us
    psum x1, blocking collectives, on_device(): lax.psum(jnp.concatenate([whole, spread_out.reshape(-1)]), ('shards', 'co...  39.9 us
    reduce_scatter x1, waiting for transfers between devices, on_device(): lax.psum_scatter(normed_part.astype(jnp.bfloat16), 'tensor', scatter_dime...  38 us
    reduce_scatter x1, waiting for transfers between devices, on_device(): lax.psum_scatter(partial_value.astype(jnp.bfloat16), 'tensor', scatter_di...  37.7 us
    unnamed x263, local copies, waits for them, and re-layouts  31.5 us
    psum x1, waiting for transfers between devices, on_device(): final_bc = lax.psum(final_back[:, inner_width + head_count:], 'tensor')  29.7 us
  transfers between devices with their start and end apart: 14, of which 11 were waited for; matrix products, arithmetic and copies ran while one was open for 18% of the time, Pallas kernels for 0%

profile of v1, /device:TPU:0, one launch (start us, length us, event | category | flops | bytes accessed | tf_op | source)
XLA Modules:
  0.0 692.0 jit_solution(17481745025074733275)
XLA Ops:
  17.8 6.8 copy.425
  31.5 6.2 multiply_convert_fusion.2
  37.6 28.4 %all-gather.4.cloned.1.call-done = bf16[768,1536]{1,0:T(8,128)(2,1)} async-done(((bf16[192,1536]{1,0:T(8,128)(2,1)}), bf16[768,1536]{1,0:T(8,128)(2,1)}) %all-gather.4.cloned.1.call-update) | async-done | bytes 2359312 | tf_op jit(solution)/shard_map/all_gather | solution.py:98
  66.0 5.9 fusion.46
  153.4 7.6 %multiply_reduce_fusion.4 = (f32[2048]{0:T(1024)S(1)}, bf16[2048,768]{0,1:T(8,128)(2,1)}) fusion(f32[2048,768]{0,1:T(8,128)} %copy.425, bf16[768,1536]{1,0:T(8,128)(2,1)} %all-gather.4.cloned.1.call-done, f32[2048,384]{1,0:T(8,128)S(1)} %get-tuple-element.168, f32[384]{0:T(512)S(1)} %copy-done.75), kind=kOutput, calls=%fused_computation.13 | convolution fusion | flops 1214248960 | bytes 13182464 | tf_op jit(solution)/shard_map/dot_general | solution.py:25
  161.6 11.4 %psum.21 = f32[2,2048]{1,0:T(2,128)} all-reduce(f32[2,2048]{1,0:T(2,128)} %pad_maximum_fusion.5), channel_id=1, replica_groups=mesh['shards'=4,'context'=2,'tensor'=4] {'tensor'}, use_global_device_ids=true, to_apply=%region_5.6 | all-reduce | flops 4096 | bytes 32768 | tf_op jit(solution)/shard_map/psum | solution.py:178
  173.9 10.1 %fusion.23 = (f32[384]{0:T(512)}, bf16[2048,384]{1,0:T(8,128)(2,1)}, bf16[2048,384]{1,0:T(8,128)(2,1)}, f32[384]{0:T(512)}) fusion(f32[2,1024,384]{2,1,0:T(8,128)} %copy.404, f32[2048,1152]{1,0:T(8,128)} %copy-done.25, f32[2048,384]{1,0:T(8,128)} %copy-done.1, f32[2048]{0:T(1024)S(1)} %fusion.106, f32[384]{0:T(512)} %convert_element_type.149, ...), kind=kOutput, calls=%fused_computation.41 | convolution fusion | flops 1227619584 | bytes 22631424 | tf_op jit(solution)/shard_map/dot_general | solution.py:21
  190.5 12.2 %fusion.4 = (f32[2,4,6,256]{3,2,1,0:T(8,128)}, f32[2,4,6,256]{3,2,1,0:T(8,128)}, f32[2,4,6,256]{3,2,1,0:T(8,128)}, f32[2,4,256,256]{3,2,1,0:T(8,128)S(1)}) fusion(f32[2,4,6,256]{3,2,1,0:T(8,128)} %copy.346, f32[2,4,6,256]{3,2,1,0:T(8,128)} %copy-done.48, f32[2,4,256,256]{3,2,1,0:T(8,128)} %copy-done.41, pred[256,256]{1,0:T(8,128)(4,1)} %iota_compare_fusion, ...), kind=kOutput, calls=%fused_computation.7 | convolution fusion | flops 442986496 | bytes 7651328 | tf_op jit(solution)/shard_map/scihp,scjhp->schij/dot_general | solution.py:232
  204.4 5.4 fusion.6
  218.7 7.1 %collective-permute-done.2 = f32[2,6,128,64]{2,3,1,0:T(8,128)S(1)} collective-permute-done((f32[2,6,128,64]{2,3,1,0:T(8,128)S(1)}, f32[2,6,128,64]{2,3,1,0:T(8,128)S(1)}, u32[]{:S(2)}, u32[]{:S(2)}) %collective-permute-start.2) | collective-permute-done | bytes 393248 | tf_op jit(solution)/shard_map/ppermute | solution.py:17
  238.0 6.6 multiply_reduce_fusion.16
  257.9 6.1 multiply_reduce_fusion.10
  272.2 5.9 fusion.35
  299.0 5.8 fusion.16
  329.5 5.5 convolution_convert_fusion
  335.1 40.1 %reduce-scatter.19.cloned.1.call-done = bf16[96,646]{1,0:T(8,128)(2,1)} async-done(((bf16[768,646]{1,0:T(8,128)(2,1)}), bf16[96,646]{1,0:T(8,128)(2,1)}) %reduce-scatter.19.cloned.1.call-update) | async-done | bytes 124048
  377.0 37.7 %reduce-scatter.9.cloned.1.call-done = bf16[512,768]{0,1:T(8,128)(2,1)} async-done(((bf16[2048,768]{0,1:T(8,128)(2,1)}), bf16[512,768]{0,1:T(8,128)(2,1)}) %reduce-scatter.9.cloned.1.call-update) | async-done | bytes 786448 | tf_op jit(solution)/shard_map/reduce_scatter | solution.py:186
  417.6 38.0 %reduce-scatter.11.cloned.1.call-done = bf16[512,768]{0,1:T(8,128)(2,1)} async-done(((bf16[2048,768]{0,1:T(8,128)(2,1)}), bf16[512,768]{0,1:T(8,128)(2,1)}) %reduce-scatter.11.cloned.1.call-update) | async-done | bytes 786448 | tf_op jit(solution)/shard_map/reduce_scatter | solution.py:288
  463.6 57.7 %reduce-scatter.15.cloned.1.call-done = bf16[96,384]{1,0:T(8,128)(2,1)} async-done(((bf16[768,384]{1,0:T(8,128)(2,1)}), bf16[96,384]{1,0:T(8,128)(2,1)}) %reduce-scatter.15.cloned.1.call-update) | async-done | bytes 73744 | tf_op jit(solution)/shard_map/reduce_scatter | solution.py:204
  522.8 62.8 %reduce-scatter.17.cloned.1.call-done = bf16[96,384]{1,0:T(8,128)(2,1)} async-done(((bf16[768,384]{1,0:T(8,128)(2,1)}), bf16[96,384]{1,0:T(8,128)(2,1)}) %reduce-scatter.17.cloned.1.call-update) | async-done | bytes 73744 | tf_op jit(solution)/shard_map/reduce_scatter | solution.py:195
  588.8 29.7 %all-reduce.3.cloned.1.call-done = f32[96,256]{0,1:T(8,128)} async-done(((f32[96,256]{0,1:T(8,128)}), f32[96,256]{0,1:T(8,128)}) %all-reduce.3.cloned.1.call-update) | async-done | bytes 98320 | tf_op jit(solution)/shard_map/psum | solution.py:316
  620.2 39.9 %psum.22 = f32[9544]{0:T(1024)S(1)} all-reduce(f32[9544]{0:T(1024)S(1)} %pad_maximum_fusion.4), channel_id=1, replica_groups=mesh['shards'=4,'context'=2,'tensor'=4] {'shards','context','tensor'}, use_global_device_ids=true, to_apply=%region_34.35 | all-reduce | flops 9544 | bytes 76352 | tf_op jit(solution)/shard_map/psum | solution.py:320
  667.9 11.6 %all-gather.8.cloned.1.call-done = bf16[2048,768]{0,1:T(8,128)(2,1)} async-done(((bf16[512,768]{0,1:T(8,128)(2,1)}), bf16[2048,768]{0,1:T(8,128)(2,1)}) %all-gather.8.cloned.1.call-update) | async-done | bytes 3145744 | tf_op jit(solution)/shard_map/all_gather | solution.py:298
  679.5 5.4 copy.430
  (438 shorter events, 222.1 us)
Async XLA Ops:
  7.2 58.8 %all-gather.4.cloned.1.call-start = ((), (), s32[]{:S(2)}) async-start(), calls=%async_computation.6 | async-start | bytes 2949120 | tf_op jit(solution)/shard_map/all_gather | solution.py:98
  12.6 297.4 %reduce-scatter.13.cloned.1.call-start = ((), (), s32[]{:S(2)}) async-start(), calls=%async_computation.10 | async-start | bytes 2621440 | tf_op jit(solution)/shard_map/reduce_scatter | solution.py:282
  31.4 46.0 %copy-start.108 = (f32[6]{0:T(128)}, f32[6]{0:T(128)S(1)}, u32[]{:S(2)}) copy-start(f32[6]{0:T(128)S(1)} %exponential_negate_fusion) | copy-start | bytes 76
  31.4 67.2 %copy-start.91 = (f32[1,256]{1,0:T(1,128)}, f32[1,256]{1,0:T(1,128)S(1)}, u32[]{:S(2)}) copy-start(f32[1,256]{1,0:T(1,128)S(1)} %get-tuple-element.206) | copy-start | bytes 3076
  31.4 67.2 %copy-start.93 = (f32[1,256]{1,0:T(1,128)}, f32[1,256]{1,0:T(1,128)S(1)}, u32[]{:S(2)}) copy-start(f32[1,256]{1,0:T(1,128)S(1)} %get-tuple-element.207) | copy-start | bytes 3076
  31.4 67.2 %copy-start.94 = (f32[1,256]{1,0:T(1,128)}, f32[1,256]{1,0:T(1,128)S(1)}, u32[]{:S(2)}) copy-start(f32[1,256]{1,0:T(1,128)S(1)} %get-tuple-element.208) | copy-start | bytes 3076
  31.4 67.2 %copy-start.95 = (f32[1,256]{1,0:T(1,128)}, f32[1,256]{1,0:T(1,128)S(1)}, u32[]{:S(2)}) copy-start(f32[1,256]{1,0:T(1,128)S(1)} %get-tuple-element.209) | copy-start | bytes 3076
  81.2 39.0 %copy-start.71 = (f32[2,1,6]{2,1,0:T(1,128)}, f32[2,1,6]{2,1,0:T(1,128)S(1)}, u32[]{:S(2)}) copy-start(f32[2,1,6]{2,1,0:T(1,128)S(1)} %get-tuple-element.203) | copy-start | bytes 148
  83.1 15.2 %collective-permute-start = (bf16[2,3,640]{1,2,0:T(8,128)(2,1)S(1)}, bf16[2,3,640]{1,2,0:T(8,128)(2,1)S(1)}, u32[]{:S(2)}, u32[]{:S(2)}) collective-permute-start(bf16[2,3,640]{1,2,0:T(8,128)(2,1)S(1)} %copy.433), channel_id=1, source_target_pairs={{0,4},{1,5},{2,6},{3,7},{8,12},{9,13},{10,14},{11,15},{16,20},{17,... | collective-permute-start | bytes 23048 | tf_op jit(solution)/shard_map/ppermute | solution.py:17
  117.7 9.9 %collective-permute-start.1 = (f32[2,6,128,64]{2,3,1,0:T(8,128)}, f32[2,6,128,64]{2,3,1,0:T(8,128)}, u32[]{:S(2)}, u32[]{:S(2)}) collective-permute-start(f32[2,6,128,64]{2,3,1,0:T(8,128)} %fusion.85), channel_id=1, source_target_pairs={{0,4},{1,5},{2,6},{3,7},{8,12},{9,13},{10,14},{11,15},{16,20},{17,... | collective-permute-start | bytes 1179656 | tf_op jit(solution)/shard_map/ppermute | solution.py:17
  213.0 12.7 %collective-permute-start.2 = (f32[2,6,128,64]{2,3,1,0:T(8,128)S(1)}, f32[2,6,128,64]{2,3,1,0:T(8,128)S(1)}, u32[]{:S(2)}, u32[]{:S(2)}) collective-permute-start(f32[2,6,128,64]{2,3,1,0:T(8,128)S(1)} %fusion.84), channel_id=1, source_target_pairs={{4,0},{5,1},{6,2},{7,3},{12,8},{13,9},{14,10},{15,11},{20,16},{21,... | collective-permute-start | bytes 1179656 | tf_op jit(solution)/shard_map/ppermute | solution.py:17
  266.6 5.6 collective-permute-start.3
  278.1 97.0 %reduce-scatter.19.cloned.1.call-start = ((), (), s32[]{:S(2)}) async-start(), calls=%async_computation.15 | async-start | bytes 1327104
  313.4 101.3 %reduce-scatter.9.cloned.1.call-start = ((), (), s32[]{:S(2)}) async-start(), calls=%async_computation.7 | async-start | bytes 3932160 | tf_op jit(solution)/shard_map/reduce_scatter | solution.py:186
  314.0 141.7 %reduce-scatter.11.cloned.1.call-start = ((), (), s32[]{:S(2)}) async-start(), calls=%async_computation.9 | async-start | bytes 3932160 | tf_op jit(solution)/shard_map/reduce_scatter | solution.py:288
  324.2 197.1 %reduce-scatter.15.cloned.1.call-start = ((), (), s32[]{:S(2)}) async-start(), calls=%async_computation.12 | async-start | bytes 663552 | tf_op jit(solution)/shard_map/reduce_scatter | solution.py:204
  329.4 256.3 %reduce-scatter.17.cloned.1.call-start = ((), (), s32[]{:S(2)}) async-start(), calls=%async_computation.14 | async-start | bytes 663552 | tf_op jit(solution)/shard_map/reduce_scatter | solution.py:195
  335.0 82.5 %copy-start.70 = (f32[1,1,2,1024]{3,2,1,0:T(2,128)S(1)}, f32[1,1,2,1024]{3,2,1,0:T(2,128)}, u32[]{:S(2)}) copy-start(f32[1,1,2,1024]{3,2,1,0:T(2,128)} %get-tuple-element.198) | copy-start | bytes 24580
  335.0 120.6 %copy-start.40 = (f32[512,256]{1,0:T(8,128)S(1)}, f32[512,256]{1,0:T(8,128)}, u32[]{:S(2)}) copy-start(f32[512,256]{1,0:T(8,128)} %reduce-scatter.13.cloned.1.call-done) | copy-start | bytes 1572868
  335.0 120.6 %copy-start.69 = (f32[768]{0:T(1024)S(1)}, f32[768]{0:T(1024)}, u32[]{:S(2)}) copy-start(f32[768]{0:T(1024)} %copy-done.68) | copy-start | bytes 9220
  335.0 283.5 %all-reduce.3.cloned.1.call-start = ((), (), s32[]{:S(2)}) async-start(), calls=%async_computation.13 | async-start | bytes 262144 | tf_op jit(solution)/shard_map/psum | solution.py:316
  376.9 286.4 %all-gather.6.cloned.1.call-start = ((), (), s32[]{:S(2)}) async-start(), calls=%async_computation.8 | async-start | bytes 3932160 | tf_op jit(solution)/shard_map/all_gather | solution.py:190
  417.5 262.0 %all-gather.8.cloned.1.call-start = ((), (), s32[]{:S(2)}) async-start(), calls=%async_computation.11 | async-start | bytes 3932160 | tf_op jit(solution)/shard_map/all_gather | solution.py:298
  458.2 129.1 %copy-start.51 = (bf16[96,646]{1,0:T(8,128)(2,1)S(1)}, bf16[96,646]{1,0:T(8,128)(2,1)}, u32[]{:S(2)}) copy-start(bf16[96,646]{1,0:T(8,128)(2,1)} %reduce-scatter.19.cloned.1.call-done) | copy-start | bytes 372100
  (111 other events, 628.5 us)
Sparse Core Ops, SparseCore 0:
  12.8 53.1 all-gather.3
  278.2 28.5 reduce-scatter.12
  313.5 61.6 reduce-scatter.18
  377.7 36.8 reduce-scatter.8
  417.6 37.9 reduce-scatter.10
  459.1 62.1 reduce-scatter.14
  524.6 61.0 reduce-scatter.16
  588.1 30.4 all-reduce.2
  620.1 28.7 all-gather.5
  650.9 28.6 all-gather.7
